TPU v7x, 512 devices: a whole 4x8x8 slice. The times are simulated.
512 devices in a mesh: mem: 16 (over y, core), reg: 32 (over z, x).
Axes of the slice: x: 4, y: 8, z: 8, core: 2. Of those that a mesh axis runs over, the one named last changes fastest.
Arguments:
- perturb: float32 [256, 512, 1024], P('mem', 'reg'), may hold values from -6 to 6
- mean_state: float32 [512, 1024], P('reg'), may hold values from -6 to 6
- obs_pert: float32 [256, 256, 256], P('mem', 'reg'), may hold values from -6 to 6
- depart: float32 [256, 256], P('reg'), may hold values from -6 to 6
- inv_var: float32 [256, 256], P('reg'), may hold values from 0.01 to 0.1
- lists: int32 [512, 12], P('reg'), may hold values from 0 to 255, as said below
- counts: int32 [512], P('reg'), may hold values from 6 to 12
Outputs:
- analysis: float32 [256, 512, 1024], P('mem', 'reg')
Inputs may be any that keep to these rules, and one draw needn't show every extreme that they name: `lists`: tile t lies in region t // 16; its list holds 12 different block ids, all from the blocks of regions t // 16 - 1, t // 16 and t // 16 + 1 (taken modulo the regions); block b belongs to region b // 8.
All inputs are finite; a program needn't handle non-finite values.
Results may differ from a plain program's by a relative error of at most 0.0003.
Values sent between devices are 32-bit elements; how exact they have to be, the bound alone decides.
A program may use at most 64 MiB of HBM per device.

v0:
```python
import jax
import jax.numpy as jnp
from jax import lax
from jax.sharding import PartitionSpec as P

ITERS = 6


def padded(block, sides, width):
    for axis, dim in sides:
        count = lax.axis_size(axis)
        forward = [(i, i + 1) for i in range(count - 1)]
        forward.append((count - 1, 0))
        backward = [(target, source) for source, target in forward]
        low = lax.ppermute(
            lax.slice_in_dim(block, block.shape[dim] - width, None, axis=dim), axis, forward
        )
        high = lax.ppermute(lax.slice_in_dim(block, 0, width, axis=dim), axis, backward)
        block = jnp.concatenate([low, block, high], axis=dim)
    return block


def tile_terms(ensemble, departures, variances, block_ids, live_count):
    members = ensemble.shape[0]
    chosen = jnp.take(ensemble, block_ids, axis=1).reshape(members, -1)
    live = (jnp.arange(block_ids.shape[0]) < live_count).astype(jnp.float32)
    weights = (jnp.take(variances, block_ids, axis=0) * live[:, None]).reshape(-1)
    values = jnp.take(departures, block_ids, axis=0).reshape(-1)
    weighted = chosen * weights[None, :]
    square = jnp.dot(
        weighted, chosen.T, precision=lax.Precision.HIGHEST, preferred_element_type=jnp.float32
    )
    vector = jnp.dot(
        weighted, values, precision=lax.Precision.HIGHEST, preferred_element_type=jnp.float32
    )
    return jnp.concatenate([square, vector[None, :]], axis=0)


def analysis_weights(term):
    members = term.shape[1]
    square = term[:members]
    vector = term[members]
    eye = jnp.eye(members, dtype=jnp.float32)
    precision_matrix = square + (members - 1.0) * eye
    scale_total = jnp.trace(precision_matrix) - (members - 1.0) * (members - 1.0)
    iterate = precision_matrix / scale_total
    inverse_root = eye
    for step in range(ITERS):
        middle = 1.5 * eye - 0.5 * jnp.dot(inverse_root, iterate, precision=lax.Precision.HIGHEST)
        iterate = jnp.dot(iterate, middle, precision=lax.Precision.HIGHEST)
        inverse_root = jnp.dot(middle, inverse_root, precision=lax.Precision.HIGHEST)
    spread_weights = jnp.sqrt((members - 1.0) / scale_total) * inverse_root
    inner = jnp.dot(inverse_root, vector, precision=lax.Precision.HIGHEST)
    mean_weights = jnp.dot(inverse_root, inner, precision=lax.Precision.HIGHEST) / scale_total
    return spread_weights + mean_weights[:, None]


def on_device(perturb, mean_state, obs_pert, depart, inv_var, lists, counts):
    group_count = lax.axis_size("mem")
    group_index = lax.axis_index("mem")
    region = lax.axis_index("reg")
    group_members, tile_group, cells = perturb.shape
    members = group_members * group_count
    per_device = tile_group // group_count
    blocks = obs_pert.shape[1]
    block_total = blocks * lax.axis_size("reg")
    stacked = jnp.concatenate([obs_pert, depart[None], inv_var[None]], axis=0)
    rimmed = padded(stacked, (("reg", 1),), blocks)
    local_ids = jnp.mod(lists - region * blocks + blocks, block_total)
    whole = lax.all_gather(rimmed, "mem", axis=0, tiled=True)
    whole = whole.reshape(group_count, group_members + 2, 3 * blocks, -1)
    ensemble = whole[:, :group_members].reshape(members, 3 * blocks, -1)
    departures = whole[0, group_members]
    variances = whole[0, group_members + 1]
    start = group_index * per_device
    own_ids = lax.dynamic_slice_in_dim(local_ids, start, per_device, 0)
    own_counts = lax.dynamic_slice_in_dim(counts, start, per_device, 0)
    terms = lax.map(
        lambda pair: tile_terms(ensemble, departures, variances, pair[0], pair[1]),
        (own_ids, own_counts),
    )
    combined = lax.map(analysis_weights, terms)
    full_members = lax.all_to_all(perturb, "mem", split_axis=1, concat_axis=0, tiled=True)
    start = group_index * per_device
    own_mean = lax.dynamic_slice_in_dim(mean_state, start, per_device, 0)
    moved = jnp.einsum(
        "qji,jqc->iqc",
        combined,
        full_members,
        precision=lax.Precision.HIGHEST,
        preferred_element_type=jnp.float32,
    )
    updated = own_mean[None, :, :] + moved
    return lax.all_to_all(updated, "mem", split_axis=0, concat_axis=1, tiled=True)


def solution(mesh):
    placed = (
        P("mem", "reg", None),
        P("reg", None),
        P("mem", "reg", None),
        P("reg", None),
        P("reg", None),
        P("reg", None),
        P("reg"),
    )
    return jax.shard_map(
        on_device, mesh=mesh, in_specs=placed, out_specs=P("mem", "reg", None), check_vma=False
    )
```

profile of v0, /device:TPU:1, one launch (start us, length us, event | category | flops | bytes accessed | tf_op | source)
XLA Modules:
  0.0 182.1 jit_solution(16645121332279169318)
XLA Ops:
  6.5 0.0 copy-start
  6.5 1.0 pad_maximum_fusion.1
  7.5 3.9 %collective-permute-start = (f32[18,8,256]{2,1,0:T(8,128)S(1)}, f32[18,8,256]{2,1,0:T(8,128)S(1)}, u32[]{:S(2)}, u32[]{:S(2)}) collective-permute-start(f32[18,8,256]{2,1,0:T(8,128)S(1)} %pad_maximum_fusion.1), channel_id=1, source_target_pairs={{0,1},{1,2},{2,3},{3,4},{4,5},{5,6},{6,7},{7,8},{8,9},{9,10},{10,1... | collective-permute-start | bytes 442376 | tf_op jit(solution)/shard_map/ppermute | solution.py:15
  11.5 11.7 %collective-permute-start.1 = (f32[18,8,256]{2,1,0:T(8,128)S(1)}, f32[18,8,256]{2,1,0:T(8,128)S(1)}, u32[]{:S(2)}, u32[]{:S(2)}) collective-permute-start(f32[18,8,256]{2,1,0:T(8,128)S(1)} %pad_maximum_fusion.1), channel_id=1, source_target_pairs={{1,0},{2,1},{3,2},{4,3},{5,4},{6,5},{7,6},{8,7},{9,8},{10,9},{11,1... | collective-permute-start | bytes 442376 | tf_op jit(solution)/shard_map/ppermute | solution.py:18
  23.2 1.6 collective-permute-done
  24.8 0.9 collective-permute-done.1
  25.7 1.7 pad_maximum_fusion
  27.4 0.0 all-gather.2.cloned.1.call-update
  27.4 2.8 %copy.13 = f32[16,16,1024]{2,0,1:T(8,128)} copy(f32[16,16,1024]{2,1,0:T(8,128)} %param.9) | data formatting | bytes 2097152 | tf_op args[0]
  30.2 8.7 %all-to-all-start = ((f32[16,16,1024]{2,0,1:T(8,128)}), f32[16,16,1024]{2,0,1:T(8,128)}, u32[]{:S(2)}, u32[]{:S(2)}) async-start(f32[16,16,1024]{2,0,1:T(8,128)} %copy.13), calls=%async_computation | async-start | bytes 2097152 | tf_op jit(solution)/shard_map/all_to_all | solution.py:83
  38.9 0.6 dynamic_slice.20
  39.6 0.0 copy-done
  39.6 0.6 compare_convert_fusion
  40.2 60.2 %all-gather.2.cloned.1.call-done = f32[288,24,256]{2,1,0:T(8,128)} async-done(((f32[18,24,256]{2,1,0:T(8,128)}), f32[288,24,256]{2,1,0:T(8,128)}) %all-gather.2.cloned.1.call-update) | async-done | bytes 7077904 | tf_op jit(solution)/shard_map/all_gather | solution.py:70
  100.4 0.8 slice_bitcast_fusion
  101.2 6.0 %slice.23 = f32[16,16,24,256]{3,2,1,0:T(8,128)} slice(f32[16,18,24,256]{3,2,1,0:T(8,128)} %bitcast.113), slice={[0:16], [0:16], [0:24], [0:256]} | slice | bytes 12582912 | tf_op jit(solution)/shard_map/slice | solution.py:72
  107.2 0.6 gather_fusion.1
  107.8 0.6 gather_fusion.2
  108.3 7.5 %copy.12 = f32[16,16,24,256]{3,1,0,2:T(8,128)} copy(f32[16,16,24,256]{3,2,1,0:T(8,128)} %slice.23) | data formatting | bytes 12582912 | tf_op jit(solution)/shard_map/slice | solution.py:72
  115.8 3.5 %gather_fusion = f32[12,256,256]{2,1,0:T(8,128)S(1)} fusion(f32[256,24,256]{2,0,1:T(8,128)} %bitcast.111, s32[1024]{0:T(1024)S(1)} %pad_clamp_fusion.1), kind=kCustom, calls=%fused_computation.2 | custom fusion | bytes 6291504 | tf_op jit(solution)/shard_map/while/body/eval_jaxpr/jit(_take)/gather | solution.py:25
  119.3 0.1 select_bitcast_fusion
  119.4 3.6 %select_reduce_fusion = (f32[]{:T(128)}, f32[256,256]{1,0:T(8,128)S(1)}) fusion(f32[12,256,256]{2,1,0:T(8,128)S(1)} %gather_fusion, pred[12]{0:T(512)(128)(4,1)S(1)} %get-tuple-element.45, f32[12,256]{1,0:T(8,128)S(1)} %get-tuple-element.36), kind=kOutput, calls=%fused_computation.40 | convolution fusion | flops 2418606080 | bytes 3420176 | tf_op jit(solution)/shard_map/while/body/eval_jaxpr/dot_general | solution.py:30
  123.6 0.3 fusion.21
  123.9 0.4 fusion.40
  124.3 0.3 fusion.37
  124.6 0.4 fusion.20
  125.0 0.4 fusion.48
  125.4 0.4 fusion.47
  125.8 0.4 fusion.19
  126.2 0.4 fusion.50
  126.6 0.4 fusion.49
  126.9 0.4 fusion.18
  127.3 0.4 fusion.52
  127.7 0.4 fusion.51
  128.1 0.7 copy-done.1
  128.8 1.1 fusion.17
  130.0 1.3 fusion.54
  131.3 1.4 fusion.53
  132.7 0.4 fusion.16
  133.1 0.6 fusion.55
  133.7 2.6 %fusion.32 = f32[256,1]{0,1:T(1,128)S(1)} fusion(f32[12,256,256]{2,1,0:T(8,128)S(1)} %gather_fusion, f32[12,256]{1,0:T(8,128)S(1)} %get-tuple-element.36, pred[12]{0:T(512)(128)(4,1)S(1)} %get-tuple-element.45, f32[12,256,1]{1,0,2:T(8,128)S(1)} %get-tuple-element.35), kind=kOutput, calls=%fused_computation.35 | convolution fusion | flops 11010048 | bytes 3171340 | tf_op jit(solution)/shard_map/while/body/eval_jaxpr/dot_general | solution.py:33
  136.3 0.3 convolution_bitcast_fusion.1
  136.6 0.3 fusion.56
  137.0 0.1 all-to-all-done
  137.0 2.3 %fusion.15 = f32[256,1,1024]{2,0,1:T(8,128)S(1)} fusion(f32[256,1024]{1,0:T(8,128)} %bitcast.21, f32[1024]{0:T(1024)S(1)} %bitcast.119, f32[256,256]{1,0:T(8,128)S(1)} %fusion.55, f32[256]{0:T(256)S(1)} %broadcast_divide_fusion.3, f32[]{:T(128)S(6)} %sqrt.4), kind=kOutput, calls=%fused_computation.19 | convolution fusion | flops 805699584 | bytes 2364420 | tf_op jit(solution)/shard_map/qji,jqc->iqc/dot_general | solution.py:86
  139.4 1.1 copy.14
  140.5 33.2 %all_to_all.33 = f32[256,1,1024]{2,1,0:T(1,128)S(1)} all-to-all(f32[256,1,1024]{2,1,0:T(1,128)S(1)} %copy.14), channel_id=1, replica_groups=mesh['mem'=16,'reg'=32] {'mem'}, dimensions={0} | all-to-all | bytes 2097152 | tf_op jit(solution)/shard_map/all_to_all | solution.py:94
  173.6 1.6 copy.20
  (14 shorter events, 0.1 us)
Async XLA Ops:
  6.5 33.1 %copy-start = (f32[16,1024]{1,0:T(8,128)S(1)}, f32[16,1024]{1,0:T(8,128)}, u32[]{:S(2)}) copy-start(f32[16,1024]{1,0:T(8,128)} %param.10) | copy-start | bytes 196612
  6.5 32.3 %copy-start.3 = (s32[16]{0:T(128)S(1)}, s32[16]{0:T(128)}, u32[]{:S(2)}) copy-start(s32[16]{0:T(128)} %param.15) | copy-start | bytes 196
  6.5 33.0 %copy-start.2 = (s32[16,12]{1,0:T(8,128)S(1)}, s32[16,12]{1,0:T(8,128)}, u32[]{:S(2)}) copy-start(s32[16,12]{1,0:T(8,128)} %param.14) | copy-start | bytes 2308
  6.5 93.9 %all-gather.2.cloned.1.call-start = ((), (), s32[]{:S(2)}) async-start(), calls=%async_computation.2 | async-start | bytes 7520256 | tf_op jit(solution)/shard_map/all_gather | solution.py:70
  7.5 17.3 %collective-permute-start = (f32[18,8,256]{2,1,0:T(8,128)S(1)}, f32[18,8,256]{2,1,0:T(8,128)S(1)}, u32[]{:S(2)}, u32[]{:S(2)}) collective-permute-start(f32[18,8,256]{2,1,0:T(8,128)S(1)} %pad_maximum_fusion.1), channel_id=1, source_target_pairs={{0,1},{1,2},{2,3},{3,4},{4,5},{5,6},{6,7},{7,8},{8,9},{9,10},{10,1... | collective-permute-start | bytes 442376 | tf_op jit(solution)/shard_map/ppermute | solution.py:15
  11.5 14.2 %collective-permute-start.1 = (f32[18,8,256]{2,1,0:T(8,128)S(1)}, f32[18,8,256]{2,1,0:T(8,128)S(1)}, u32[]{:S(2)}, u32[]{:S(2)}) collective-permute-start(f32[18,8,256]{2,1,0:T(8,128)S(1)} %pad_maximum_fusion.1), channel_id=1, source_target_pairs={{1,0},{2,1},{3,2},{4,3},{5,4},{6,5},{7,6},{8,7},{9,8},{10,9},{11,1... | collective-permute-start | bytes 442376 | tf_op jit(solution)/shard_map/ppermute | solution.py:18
  30.2 106.8 %all-to-all-start = ((f32[16,16,1024]{2,0,1:T(8,128)}), f32[16,16,1024]{2,0,1:T(8,128)}, u32[]{:S(2)}, u32[]{:S(2)}) async-start(f32[16,16,1024]{2,0,1:T(8,128)} %copy.13), calls=%async_computation | async-start | bytes 2097152 | tf_op jit(solution)/shard_map/all_to_all | solution.py:83
  128.1 0.7 copy-start.1
Sparse Core Ops, SparseCore 0:
  27.5 72.8 all-gather.1
where the time goes:
time: 183 us; the launch traced here: 182 us
  waiting for transfers between devices  62.7 us (34%)
  blocking collectives  33.2 us (18%)
  local copies, waits for them, and re-layouts  25.7 us (14%)
  starting transfers between devices  24.3 us (13%)
  matrix products  18.4 us (10%)
  between operations  14.3 us (8%)
  other arithmetic  3.46 us (2%)
    all_gather x1, waiting for transfers between devices, on_device(): whole = lax.all_gather(rimmed, 'mem', axis=0, tiled=True)  60.2 us
    all_to_all x1, blocking collectives, on_device(): lax.all_to_all(updated, 'mem', split_axis=0, concat_axis=1, tiled=True)  33.2 us
    slice x2, local copies, waits for them, and re-layouts, on_device(): ensemble = whole[:, :group_members].reshape(members, 3 * blocks, -1)  13.5 us
    ppermute x1, starting transfers between devices, padded(): lax.ppermute(lax.slice_in_dim(block, 0, width, axis=dim), axis, backward)  11.7 us
    all_to_all x1, starting transfers between devices, on_device(): lax.all_to_all(perturb, 'mem', split_axis=1, concat_axis=0, tiled=True)  8.66 us
    ppermute x1, starting transfers between devices, padded(): lax.ppermute(lax.slice_in_dim(block, block.shape[dim] - width, None, axis...  3.95 us
  transfers between devices with their start and end apart: 4, of which 4 were waited for; matrix products, arithmetic and copies ran while one was open for 22% of the time, Pallas kernels for 0%

commit v1 on v0

v1 whole, which is shorter than its diff:
```python
import functools

import jax
import jax.numpy as jnp
from jax import lax
from jax.experimental import pallas as pl
from jax.experimental.pallas import tpu as pltpu
from jax.sharding import PartitionSpec as P

ITERS = 6
PLAN = ((), (1, 7, 0), (4,), (2, 6), (3, 5))

MESH = pl.DeviceIdType.MESH
NT = (((1,), (1,)), ((), ()))
NN = (((1,), (0,)), ((), ()))


def split(a):
    hi = a.astype(jnp.bfloat16)
    return hi, (a - hi.astype(jnp.float32)).astype(jnp.bfloat16)


def dot3(a, b, dims=NN):
    def one(x, y):
        return lax.dot_general(x, y, dims, preferred_element_type=jnp.float32)

    return one(a[0], b[0]) + (one(a[0], b[1]) + one(a[1], b[0]))


def kernel(
    n,
    regions,
    counts_in,
    lists_in,
    obs_in,
    depart_in,
    inv_in,
    mean_in,
    perturb_ref,
    out_ref,
    counts_ref,
    lists_ref,
    obs_ref,
    depart_ref,
    inv_ref,
    mean_ref,
    xa,
    cp,
    pr,
    cf,
    cs,
    ex,
    sp,
    sr,
    xin,
    og,
    hi_ref,
    lo_ref,
    send_sem,
    recv_sem,
    near_send,
    near_recv,
    pair_send,
    pair_recv,
    local_sem,
    group_in,
    near_in,
):
    me = lax.axis_index("mem")
    region = lax.axis_index("reg")
    right = lax.rem(region + 1, regions)
    left = lax.rem(region + regions - 1, regions)
    blocks = depart_in.shape[0]
    group = obs_in.shape[0]
    members = n * group
    half = members // 2
    others = n - 1
    chips = n // 2
    chip = me // 2
    core = lax.rem(me, 2)

    def partner(j):
        return 2 * lax.rem(chip + j // 2, chips) + lax.rem(core + lax.rem(j, 2), 2)

    def place(i):
        pair = i // 2
        ahead = chips // 2 + ((pair + 1) // 2) * (1 - 2 * lax.rem(pair, 2))
        return 2 * ahead + 1 - lax.rem(i, 2)

    def exchange(phase, source, target):
        def copy(j):
            to = partner(j)
            return pltpu.make_async_remote_copy(
                src_ref=source(to),
                dst_ref=target(me),
                send_sem=send_sem.at[phase, j],
                recv_sem=recv_sem.at[phase, j],
                device_id=(to, region),
                device_id_type=MESH,
            )

        return copy

    def each(action):
        def body(i, carry):
            action(place(i))
            return carry

        lax.fori_loop(0, others, body, 0)

    def each_now(action):
        for i in range(others):
            pair = i // 2
            ahead = chips // 2 + ((pair + 1) // 2) * (1 - 2 * (pair % 2))
            action(2 * ahead + 1 - i % 2)

    def near(slot, source, low, high):
        first = pltpu.make_async_remote_copy(
            src_ref=source,
            dst_ref=low,
            send_sem=near_send.at[slot],
            recv_sem=near_recv.at[slot],
            device_id=(me, right),
            device_id_type=MESH,
        )
        second = pltpu.make_async_remote_copy(
            src_ref=source,
            dst_ref=high,
            send_sem=near_send.at[slot + 1],
            recv_sem=near_recv.at[slot + 1],
            device_id=(me, left),
            device_id_type=MESH,
        )
        return first, second

    leads = me == 0
    follows = me != 0
    barrier = pltpu.get_barrier_semaphore()

    def greet(j):
        to = partner(j)

        @pl.when(to != 0)
        def _():
            pl.semaphore_signal(
                barrier, inc=1, device_id=(to, region), device_id_type=MESH
            )

    each(greet)

    loads = [
        pltpu.make_async_copy(source, target, local_sem.at[3 + at])
        for at, (source, target) in enumerate(
            (
                (counts_in, counts_ref),
                (lists_in, lists_ref),
                (obs_in, obs_ref),
                (depart_in, depart_ref),
                (inv_in, inv_ref),
                (mean_in.at[pl.ds(me, 1)], mean_ref),
            )
        )
    ]
    for load in loads:
        load.start()
    own_background = pltpu.make_async_copy(
        perturb_ref.at[:, me, :], xin.at[me], local_sem.at[1]
    )
    own_background.start()
    background = exchange(
        3, lambda to: perturb_ref.at[:, to, :], lambda slot: xin.at[slot]
    )

    @pl.when(follows)
    def _():
        pl.semaphore_wait(barrier, others)

    @pl.when(me == 1)
    def _():
        pl.semaphore_signal(
            group_in, inc=1, device_id=(0, region), device_id_type=MESH
        )
        for side in (left, right):
            pl.semaphore_signal(
                barrier, inc=1, device_id=(0, side), device_id_type=MESH
            )

    @pl.when(leads)
    def _():
        pl.semaphore_wait(group_in, 1)

    def piece(to):
        return obs_in.at[
            :, to // 2, pl.ds(pl.multiple_of(lax.rem(to, 2) * 128, 128), 128)
        ]

    obs_copy = exchange(0, piece, lambda slot: xa.at[slot])

    def send_background(point):
        for ahead in PLAN[point]:
            for flip in (0, 1):
                if ahead or flip:
                    background(2 * ahead + flip).start()

    send_background(0)
    each_now(lambda j: obs_copy(j).start())
    own_obs = pltpu.make_async_copy(piece(me), xa.at[me], local_sem.at[0])
    own_obs.start()
    send_background(1)
    for load in loads:
        load.wait()

    tile_row = lax.broadcasted_iota(jnp.int32, (n, 128), 0)
    lane = lax.broadcasted_iota(jnp.int32, (n, 128), 1)
    live = jnp.zeros((n, 128), jnp.int32)
    for t in range(n):
        live = jnp.where(tile_row == t, counts_ref[t], live)
    total = blocks * regions
    local = lax.rem(lists_ref[...] - region * blocks + (blocks + total), total)
    chosen = jnp.zeros((n, 128), jnp.float32)
    for j in range(lists_ref.shape[1]):
        hit = (lane == local[:, j : j + 1]) & (live > j)
        chosen = jnp.where(hit, 1.0, chosen)
    chosen = chosen[:, : 3 * blocks].astype(jnp.bfloat16)

    weights = inv_ref[...]
    weighted_departures = weights * depart_ref[...]
    extra_lane = lax.broadcasted_iota(jnp.int32, (blocks, 128), 1)
    extras = jnp.zeros((blocks, 128), jnp.float32)
    for i in range(group):
        one = obs_ref[i]
        vector = jnp.sum(one * weighted_departures, axis=1, keepdims=True)
        diagonal = jnp.sum(one * one * weights, axis=1, keepdims=True)
        extras = jnp.where(extra_lane == i, vector, extras)
        extras = jnp.where(extra_lane == group + i, diagonal, extras)
    ex[1] = extras

    def combine(values):
        top = values.astype(jnp.bfloat16)
        rest = values - top.astype(jnp.float32)
        middle = rest.astype(jnp.bfloat16)
        last = (rest - middle.astype(jnp.float32)).astype(jnp.bfloat16)
        parts = [
            jnp.dot(chosen, part, preferred_element_type=jnp.float32)
            for part in (top, middle, last)
        ]
        return parts[0] + (parts[1] + parts[2])

    own_obs.wait()
    each(lambda j: obs_copy(j).wait_recv())
    x = xa[...].reshape(members, 128)
    block_row = lax.broadcasted_iota(jnp.int32, weights.shape, 0)
    w = jnp.sum(
        jnp.where(block_row == me // 2, weights, 0.0), axis=0, keepdims=True
    )
    w = jnp.where(lax.rem(me, 2) == 0, w[:, :128], w[:, 128:])
    square = dot3(split(x * w), split(x), NT)
    row = lax.broadcasted_iota(jnp.int32, (half, half), 0)
    column = lax.broadcasted_iota(jnp.int32, (half, half), 1)
    cp[0] = square[:half, half:].reshape(n, group // 2, 128)
    cp[1] = jnp.where(
        row >= column, square[:half, :half], square[half:, half:]
    ).reshape(n, group // 2, 128)
    pair_copy = pltpu.make_async_remote_copy(
        src_ref=cp.at[1 - core],
        dst_ref=pr,
        send_sem=pair_send,
        recv_sem=pair_recv,
        device_id=(2 * chip + 1 - core, region),
        device_id_type=MESH,
    )
    pair_copy.start()
    pair_copy.wait_recv()
    cf[...] = cp[core] + pr[...]
    square_copy = exchange(
        1, lambda to: cf.at[to], lambda slot: cs.at[1, slot // 2, lax.rem(slot, 2)]
    )
    each_now(lambda j: square_copy(j).start())
    send_background(2)
    cs[1, chip, core] = cf[me]

    def pass_word(j):
        pl.semaphore_signal(
            near_in, inc=1, device_id=(partner(j), region), device_id_type=MESH
        )

    @pl.when(leads)
    def _():
        pl.semaphore_wait(barrier, 2)
        each_now(pass_word)

    @pl.when(follows)
    def _():
        pl.semaphore_wait(near_in, 1)

    extra_near = near(0, ex.at[1], ex.at[0], ex.at[2])
    for copy in extra_near:
        copy.start()

    def near_square(b, at):
        return near(
            2 + 2 * at, cs.at[1, b], cs.at[0, b], cs.at[2, b]
        )

    def pass_on(at, carry):
        ahead = chips // 2 + ((at + 1) // 2) * (1 - 2 * lax.rem(at, 2))

        @pl.when(ahead != 0)
        def _():
            square_copy(2 * ahead).wait_recv()

        square_copy(2 * ahead + 1).wait_recv()
        for copy in near_square(lax.rem(chip - ahead + chips, chips), at):
            copy.start()
        return carry

    lax.fori_loop(0, chips, pass_on, 0)
    send_background(3)

    def take_near(at, carry):
        for copy in near_square(at, at):
            copy.wait_recv()
        return carry

    lax.fori_loop(0, chips, take_near, 0)
    for copy in extra_near:
        copy.wait_recv()
    sp[:, group, :] = combine(ex[...].reshape(3 * blocks, 128))
    near_squares = jnp.concatenate(
        [
            cs[:, :, i // 8, i % 8, :].reshape(3 * blocks, 128)
            for i in range(group)
        ],
        axis=1,
    )
    tile_squares = combine(near_squares)
    for i in range(group):
        sp[:, i, :] = tile_squares[:, i * 128 : (i + 1) * 128]
    used = pl.ds(0, group + 1)
    tile_copy = exchange(
        2, lambda to: sp.at[to, used], lambda slot: sr.at[slot, used]
    )
    each_now(lambda j: tile_copy(j).start())
    sr[pl.ds(me, 1)] = sp[pl.ds(me, 1)]
    send_background(4)

    each(lambda j: tile_copy(j).wait_recv())
    got = sr[:, group, :]
    got_lane = lax.broadcasted_iota(jnp.int32, got.shape, 1)

    def spread_out(values):
        kept = jnp.where(got_lane < group, values, 0.0)
        per_row = 128 // group
        return jnp.concatenate(
            [
                jnp.sum(
                    pltpu.roll(
                        kept[at : at + per_row], 0, 1, stride=group, stride_axis=0
                    ),
                    axis=0,
                    keepdims=True,
                )
                for at in range(0, n, per_row)
            ],
            axis=1,
        )

    vector = spread_out(got)
    diagonal = spread_out(pltpu.roll(got, 128 - group, 1))
    scale_total = jnp.sum(diagonal, axis=1, keepdims=True) + (members - 1.0)
    inverse_scale = 1.0 / scale_total

    corner = sr[:, : group // 2].reshape(half, 128)
    both = sr[:, group // 2 : group].reshape(half, 128)
    flipped = both.T
    lower = jnp.where(row > column, both, flipped)
    upper = jnp.where(row < column, both, flipped)
    full = jnp.concatenate(
        [
            jnp.concatenate([lower, corner], axis=1),
            jnp.concatenate([corner.T, upper], axis=1),
        ],
        axis=0,
    )
    full_row = lax.broadcasted_iota(jnp.int32, (members, members), 0)
    full_column = lax.broadcasted_iota(jnp.int32, (members, members), 1)
    on_diagonal = full_row == full_column
    full = jnp.where(on_diagonal, diagonal + (members - 1.0), full) * inverse_scale

    def middle_of(product):
        return jnp.where(on_diagonal, 1.5, 0.0) - 0.5 * product

    def store(where, values):
        hi, lo = split(values)
        hi_ref[where] = hi
        lo_ref[where] = lo

    top, bottom = pl.ds(0, members), pl.ds(members, members)

    def product():
        return dot3(
            (hi_ref[bottom], lo_ref[bottom]), (hi_ref[top], lo_ref[top])
        )

    first = middle_of(full)
    store(top, dot3(split(full), split(first)))
    store(bottom, first)

    def iterate(step, carry):
        middle = split(middle_of(product()))
        store(pl.ds(0, 2 * members), dot3((hi_ref[...], lo_ref[...]), middle))
        return carry

    lax.fori_loop(1, ITERS - 1, iterate, 0)
    middle = split(middle_of(product()))
    inverse_root = dot3((hi_ref[bottom], lo_ref[bottom]), middle)
    root_parts = split(inverse_root)
    inner = dot3(split(jnp.broadcast_to(vector, (8, members))), root_parts)
    shift = dot3(split(inner), root_parts)[0:1] * inverse_scale
    spread = jnp.sqrt((members - 1.0) * inverse_scale)
    combined = split(inverse_root * spread + shift)

    own_background.wait()
    each(lambda j: background(j).wait_recv())
    values = split(xin[...].reshape(members, xin.shape[2]))
    mean = mean_ref[...]
    og[...] = (dot3(combined, values) + mean).reshape(og.shape)
    result_copy = exchange(
        4, lambda to: og.at[to], lambda slot: out_ref.at[:, slot, :]
    )
    each_now(lambda j: result_copy(j).start())
    own_result = pltpu.make_async_copy(
        og.at[me], out_ref.at[:, me, :], local_sem.at[2]
    )
    own_result.start()
    own_result.wait()
    for copy in extra_near:
        copy.wait_send()
    pair_copy.wait_send()

    def near_sent(at, carry):
        for copy in near_square(at, at):
            copy.wait_send()
        return carry

    lax.fori_loop(0, chips, near_sent, 0)
    for copies in (obs_copy, square_copy, tile_copy, background):
        each(lambda j: copies(j).wait_send())
    each(lambda j: result_copy(j).wait())


def on_device(n, regions, perturb, mean_state, obs_pert, depart, inv_var, lists, counts):
    group, tiles, cells = perturb.shape
    blocks = depart.shape[0]
    members = n * group
    f32 = jnp.float32
    hbm = pl.BlockSpec(memory_space=pltpu.HBM)
    return pl.pallas_call(
        functools.partial(kernel, n, regions),
        out_shape=jax.ShapeDtypeStruct((group, tiles, cells), f32),
        in_specs=[hbm] * 7,
        out_specs=pl.BlockSpec(memory_space=pl.ANY),
        scratch_shapes=[
            pltpu.SMEM(counts.shape, jnp.int32),
            pltpu.VMEM(lists.shape, jnp.int32),
            pltpu.VMEM(obs_pert.shape, f32),
            pltpu.VMEM(depart.shape, f32),
            pltpu.VMEM(inv_var.shape, f32),
            pltpu.VMEM((1, cells), f32),
            pltpu.VMEM((n, group, 128), f32),
            pltpu.VMEM((2, n, group // 2, 128), f32),
            pltpu.VMEM((n, group // 2, 128), f32),
            pltpu.VMEM((n, group // 2, 128), f32),
            pltpu.VMEM((3, blocks, 2, group // 2, 128), f32),
            pltpu.VMEM((3, blocks, 128), f32),
            pltpu.VMEM((n, group + 8, 128), f32),
            pltpu.VMEM((n, group + 8, 128), f32),
            pltpu.VMEM((n, group, cells), f32),
            pltpu.VMEM((n, group, cells), f32),
            pltpu.VMEM((2 * members, members), jnp.bfloat16),
            pltpu.VMEM((2 * members, members), jnp.bfloat16),
            pltpu.SemaphoreType.DMA((5, n)),
            pltpu.SemaphoreType.DMA((5, n)),
            pltpu.SemaphoreType.DMA((2 + 2 * blocks,)),
            pltpu.SemaphoreType.DMA((2 + 2 * blocks,)),
            pltpu.SemaphoreType.DMA,
            pltpu.SemaphoreType.DMA,
            pltpu.SemaphoreType.DMA((9,)),
            pltpu.SemaphoreType.REGULAR,
            pltpu.SemaphoreType.REGULAR,
        ],
        compiler_params=pltpu.CompilerParams(
            collective_id=0, has_side_effects=True, vmem_limit_bytes=32 * 2**20
        ),
        name="analysis",
    )(
        *[
            pltpu.with_memory_space_constraint(value, pltpu.HBM)
            for value in (counts, lists, obs_pert, depart, inv_var, mean_state, perturb)
        ]
    )


def solution(mesh):
    placed = (
        P("mem", "reg", None),
        P("reg", None),
        P("mem", "reg", None),
        P("reg", None),
        P("reg", None),
        P("reg", None),
        P("reg"),
    )
    return jax.shard_map(
        functools.partial(on_device, mesh.shape["mem"], mesh.shape["reg"]),
        mesh=mesh,
        in_specs=placed,
        out_specs=P("mem", "reg", None),
        check_vma=False,
    )
```

time: 183 us -> 74.6 us (0.41)
  Pallas kernels: 0 us -> 73.4 us
  waiting for transfers between devices: 62.7 us -> 0 us
  blocking collectives: 33.2 us -> 0 us
  local copies, waits for them, and re-layouts: 25.7 us -> 0.97 us
  starting transfers between devices: 24.3 us -> 0 us
  matrix products: 18.4 us -> 0 us
  between operations: 14.3 us -> 0.01 us
  other arithmetic: 3.46 us -> 0 us
    pallas_call x0 -> x1, Pallas kernels: none -> 73.4 us  [on_device(): pl.pallas_call(functools.partial(kernel, n, regions), out_shape=jax.Shape...]
    all_gather x1 -> x0, waiting for transfers between devices: 60.2 us -> none  [on_device(): whole = lax.all_gather(rimmed, 'mem', axis=0, tiled=True)]
    all_to_all x1 -> x0, blocking collectives: 33.2 us -> none  [on_device(): lax.all_to_all(updated, 'mem', split_axis=0, concat_axis=1, tiled=True)]
    dot_general x22 -> x0, matrix products: 18.4 us -> none  [the longest x1 3.64 us: tile_terms(): jnp.dot(weighted, chosen.T, precision=lax.Precision.HIGHEST, preferred_el...]
    ppermute x2 -> x0, starting transfers between devices: 15.6 us -> none  [the longest x1 11.7 us: padded(): lax.ppermute(lax.slice_in_dim(block, 0, width, axis=dim), axis, backward)]
    slice x2 -> x0, local copies, waits for them, and re-layouts: 13.5 us -> none  [on_device(): ensemble = whole[:, :group_members].reshape(members, 3 * blocks, -1)]
    all_to_all x1 -> x0, starting transfers between devices: 8.66 us -> none  [on_device(): lax.all_to_all(perturb, 'mem', split_axis=1, concat_axis=0, tiled=True)]
    gather x3 -> x0, local copies, waits for them, and re-layouts: 4.67 us -> none  [the longest x1 3.53 us: tile_terms(): chosen = jnp.take(ensemble, block_ids, axis=1).reshape(members, -1)]
  transfers between devices with their start and end apart: 4 -> 0, of which waited for: 4 -> 0; matrix products, arithmetic and copies ran while one was open for 22% -> 0% of each run, Pallas kernels for 0% -> 0%
where the time goes in v1:
time: 74.6 us; the launch traced here: 74.4 us
  Pallas kernels  73.4 us (98%)
  local copies, waits for them, and re-layouts  0.97 us (1%)
    pallas_call x1, Pallas kernels, on_device(): pl.pallas_call(functools.partial(kernel, n, regions), out_shape=jax.Shape...  73.4 us

profile of v1, /device:TPU:1, one launch (start us, length us, event | category | flops | bytes accessed | tf_op | source)
XLA Modules:
  0.0 74.4 jit_solution(12918520378744337011)
XLA Ops:
  0.0 73.4 %analysis.1 = f32[16,16,1024]{2,1,0:T(8,128)S(1)} custom-call(s32[16]{0:T(128)} %counts_in.1, s32[16,12]{1,0:T(8,128)} %lists_in.1, f32[16,8,256]{2,1,0:T(8,128)} %obs_in.1, f32[8,256]{1,0:T(8,128)} %depart_in.1, f32[8,256]{1,0:T(8,128)} %inv_in.1, f32[16,1024]{1,0:T(8,128)} %mean_in.1, f32[16,16,1024]{2,1,0:T(8,128)} %perturb_ref.1), custom_call_target="tpu_custom_call" | custom-call | tf_op jit(solution)/shard_map/analysis/pallas_call | solution.py:458
  73.4 1.0 %copy.9 = f32[16,16,1024]{2,1,0:T(8,128)} copy(f32[16,16,1024]{2,1,0:T(8,128)S(1)} %analysis.1) | data formatting | bytes 2097152

commit v2 on v1

--- a/solution.py
+++ b/solution.py
@@ -8,7 +8,9 @@
 from jax.sharding import PartitionSpec as P
 
 ITERS = 6
-PLAN = ((), (1, 7, 0), (4,), (2, 6), (3, 5))
+PLAN = ((), (4,), (2, 6), (1, 7, 0), (3, 5))
+FIRST = ((), (3, 5), (4,), (1, 7, 0), (2, 6))
+LAST = ((), (4,), (), (1, 7, 0, 2, 6), (3, 5))
 
 MESH = pl.DeviceIdType.MESH
 NT = (((1,), (1,)), ((), ()))
@@ -58,6 +60,7 @@
     lo_ref,
     send_sem,
     recv_sem,
+    chip_sem,
     near_send,
     near_recv,
     pair_send,
@@ -82,37 +85,35 @@
     def partner(j):
         return 2 * lax.rem(chip + j // 2, chips) + lax.rem(core + lax.rem(j, 2), 2)
 
-    def place(i):
-        pair = i // 2
-        ahead = chips // 2 + ((pair + 1) // 2) * (1 - 2 * lax.rem(pair, 2))
-        return 2 * ahead + 1 - lax.rem(i, 2)
-
-    def exchange(phase, source, target):
+    def exchange(phase, source, target, arrival=None):
         def copy(j):
             to = partner(j)
+            landed = recv_sem.at[phase] if arrival is None else arrival(j)
             return pltpu.make_async_remote_copy(
                 src_ref=source(to),
                 dst_ref=target(me),
-                send_sem=send_sem.at[phase, j],
-                recv_sem=recv_sem.at[phase, j],
+                send_sem=send_sem.at[phase],
+                recv_sem=landed,
                 device_id=(to, region),
                 device_id_type=MESH,
             )
 
         return copy
 
+    def take(ref, sem):
+        pltpu.make_async_copy(ref, ref, sem).wait()
+
+    all_but_one = pl.ds(0, others)
+
+    chip_order = [
+        chips // 2 + (i + 1) // 2 * (1 - 2 * (i % 2)) for i in range(chips)
+    ]
+
     def each(action):
-        def body(i, carry):
-            action(place(i))
-            return carry
-
-        lax.fori_loop(0, others, body, 0)
-
-    def each_now(action):
-        for i in range(others):
-            pair = i // 2
-            ahead = chips // 2 + ((pair + 1) // 2) * (1 - 2 * (pair % 2))
-            action(2 * ahead + 1 - i % 2)
+        for ahead in chip_order:
+            for flip in (1, 0):
+                if ahead or flip:
+                    action(2 * ahead + flip)
 
     def near(slot, source, low, high):
         first = pltpu.make_async_remote_copy(
@@ -197,13 +198,24 @@
     obs_copy = exchange(0, piece, lambda slot: xa.at[slot])
 
     def send_background(point):
-        for ahead in PLAN[point]:
-            for flip in (0, 1):
-                if ahead or flip:
-                    background(2 * ahead + flip).start()
+        begins, ends = region == 0, region == regions - 1
+        for here, plan in (
+            (begins, FIRST),
+            (ends, LAST),
+            (jnp.logical_not(begins | ends), PLAN),
+        ):
+            if not plan[point]:
+                continue
+
+            @pl.when(here)
+            def _(plan=plan):
+                for ahead in plan[point]:
+                    for flip in (0, 1):
+                        if ahead or flip:
+                            background(2 * ahead + flip).start()
 
     send_background(0)
-    each_now(lambda j: obs_copy(j).start())
+    each(lambda j: obs_copy(j).start())
     own_obs = pltpu.make_async_copy(piece(me), xa.at[me], local_sem.at[0])
     own_obs.start()
     send_background(1)
@@ -247,7 +259,7 @@
         return parts[0] + (parts[1] + parts[2])
 
     own_obs.wait()
-    each(lambda j: obs_copy(j).wait_recv())
+    take(xa.at[all_but_one], recv_sem.at[0])
     x = xa[...].reshape(members, 128)
     block_row = lax.broadcasted_iota(jnp.int32, weights.shape, 0)
     w = jnp.sum(
@@ -273,9 +285,12 @@
     pair_copy.wait_recv()
     cf[...] = cp[core] + pr[...]
     square_copy = exchange(
-        1, lambda to: cf.at[to], lambda slot: cs.at[1, slot // 2, lax.rem(slot, 2)]
-    )
-    each_now(lambda j: square_copy(j).start())
+        1,
+        lambda to: cf.at[to],
+        lambda slot: cs.at[1, slot // 2, lax.rem(slot, 2)],
+        lambda j: chip_sem.at[j // 2],
+    )
+    each(lambda j: square_copy(j).start())
     send_background(2)
     cs[1, chip, core] = cf[me]
 
@@ -287,7 +302,7 @@
     @pl.when(leads)
     def _():
         pl.semaphore_wait(barrier, 2)
-        each_now(pass_word)
+        each(pass_word)
 
     @pl.when(follows)
     def _():
@@ -297,32 +312,15 @@
     for copy in extra_near:
         copy.start()
 
-    def near_square(b, at):
-        return near(
-            2 + 2 * at, cs.at[1, b], cs.at[0, b], cs.at[2, b]
-        )
-
-    def pass_on(at, carry):
-        ahead = chips // 2 + ((at + 1) // 2) * (1 - 2 * lax.rem(at, 2))
-
-        @pl.when(ahead != 0)
-        def _():
-            square_copy(2 * ahead).wait_recv()
-
-        square_copy(2 * ahead + 1).wait_recv()
-        for copy in near_square(lax.rem(chip - ahead + chips, chips), at):
+    for ahead in chip_order:
+        take(cs.at[1, 0] if ahead else cs.at[1, 0, 0], chip_sem.at[ahead])
+        b = lax.rem(chip - ahead + chips, chips)
+        for copy in near(2, cs.at[1, b], cs.at[0, b], cs.at[2, b]):
             copy.start()
-        return carry
-
-    lax.fori_loop(0, chips, pass_on, 0)
     send_background(3)
 
-    def take_near(at, carry):
-        for copy in near_square(at, at):
-            copy.wait_recv()
-        return carry
-
-    lax.fori_loop(0, chips, take_near, 0)
+    take(cs.at[0], near_recv.at[2])
+    take(cs.at[2], near_recv.at[3])
     for copy in extra_near:
         copy.wait_recv()
     sp[:, group, :] = combine(ex[...].reshape(3 * blocks, 128))
@@ -340,11 +338,11 @@
     tile_copy = exchange(
         2, lambda to: sp.at[to, used], lambda slot: sr.at[slot, used]
     )
-    each_now(lambda j: tile_copy(j).start())
+    each(lambda j: tile_copy(j).start())
     sr[pl.ds(me, 1)] = sp[pl.ds(me, 1)]
     send_background(4)
 
-    each(lambda j: tile_copy(j).wait_recv())
+    take(sr.at[all_but_one, used], recv_sem.at[2])
     got = sr[:, group, :]
     got_lane = lax.broadcasted_iota(jnp.int32, got.shape, 1)
 
@@ -421,14 +419,14 @@
     combined = split(inverse_root * spread + shift)
 
     own_background.wait()
-    each(lambda j: background(j).wait_recv())
+    take(xin.at[all_but_one], recv_sem.at[3])
     values = split(xin[...].reshape(members, xin.shape[2]))
     mean = mean_ref[...]
     og[...] = (dot3(combined, values) + mean).reshape(og.shape)
     result_copy = exchange(
         4, lambda to: og.at[to], lambda slot: out_ref.at[:, slot, :]
     )
-    each_now(lambda j: result_copy(j).start())
+    each(lambda j: result_copy(j).start())
     own_result = pltpu.make_async_copy(
         og.at[me], out_ref.at[:, me, :], local_sem.at[2]
     )
@@ -438,15 +436,14 @@
         copy.wait_send()
     pair_copy.wait_send()
 
-    def near_sent(at, carry):
-        for copy in near_square(at, at):
-            copy.wait_send()
-        return carry
-
-    lax.fori_loop(0, chips, near_sent, 0)
-    for copies in (obs_copy, square_copy, tile_copy, background):
-        each(lambda j: copies(j).wait_send())
-    each(lambda j: result_copy(j).wait())
+    take(cs.at[0], near_send.at[2])
+    take(cs.at[2], near_send.at[3])
+    take(xa.at[all_but_one], send_sem.at[0])
+    take(cf.at[all_but_one], send_sem.at[1])
+    take(sp.at[all_but_one, used], send_sem.at[2])
+    take(xin.at[all_but_one], send_sem.at[3])
+    take(og.at[all_but_one], send_sem.at[4])
+    take(og.at[all_but_one], recv_sem.at[4])
 
 
 def on_device(n, regions, perturb, mean_state, obs_pert, depart, inv_var, lists, counts):
@@ -479,10 +476,11 @@
             pltpu.VMEM((n, group, cells), f32),
             pltpu.VMEM((2 * members, members), jnp.bfloat16),
             pltpu.VMEM((2 * members, members), jnp.bfloat16),
-            pltpu.SemaphoreType.DMA((5, n)),
-            pltpu.SemaphoreType.DMA((5, n)),
-            pltpu.SemaphoreType.DMA((2 + 2 * blocks,)),
-            pltpu.SemaphoreType.DMA((2 + 2 * blocks,)),
+            pltpu.SemaphoreType.DMA((5,)),
+            pltpu.SemaphoreType.DMA((5,)),
+            pltpu.SemaphoreType.DMA((n // 2,)),
+            pltpu.SemaphoreType.DMA((4,)),
+            pltpu.SemaphoreType.DMA((4,)),
             pltpu.SemaphoreType.DMA,
             pltpu.SemaphoreType.DMA,
             pltpu.SemaphoreType.DMA((9,)),

time: 74.6 us -> 72 us (0.965)
  Pallas kernels: 73.4 us -> 70.8 us
    pallas_call x1, Pallas kernels: 73.4 us -> 70.8 us  [on_device(): pl.pallas_call(functools.partial(kernel, n, regions), out_shape=jax.Shape...]
where the time goes in v2:
time: 72 us; the launch traced here: 71.8 us
  Pallas kernels  70.8 us (98%)
  local copies, waits for them, and re-layouts  0.97 us (1%)
    pallas_call x1, Pallas kernels, on_device(): pl.pallas_call(functools.partial(kernel, n, regions), out_shape=jax.Shape...  70.8 us

profile of v2, /device:TPU:1, one launch (start us, length us, event | category | flops | bytes accessed | tf_op | source)
XLA Modules:
  0.0 71.8 jit_solution(9658297282337215076)
XLA Ops:
  0.0 70.8 %analysis.1 = f32[16,16,1024]{2,1,0:T(8,128)S(1)} custom-call(s32[16]{0:T(128)} %counts_in.1, s32[16,12]{1,0:T(8,128)} %lists_in.1, f32[16,8,256]{2,1,0:T(8,128)} %obs_in.1, f32[8,256]{1,0:T(8,128)} %depart_in.1, f32[8,256]{1,0:T(8,128)} %inv_in.1, f32[16,1024]{1,0:T(8,128)} %mean_in.1, f32[16,16,1024]{2,1,0:T(8,128)} %perturb_ref.1), custom_call_target="tpu_custom_call" | custom-call | tf_op jit(solution)/shard_map/analysis/pallas_call | solution.py:455
  70.8 1.0 %copy.9 = f32[16,16,1024]{2,1,0:T(8,128)} copy(f32[16,16,1024]{2,1,0:T(8,128)S(1)} %analysis.1) | data formatting | bytes 2097152

commit v3 on v2

--- a/solution.py
+++ b/solution.py
@@ -9,7 +9,7 @@
 
 ITERS = 6
 PLAN = ((), (4,), (2, 6), (1, 7, 0), (3, 5))
-FIRST = ((), (3, 5), (4,), (1, 7, 0), (2, 6))
+FIRST = ((), (3, 5), (4, 1, 7, 0), (), (2, 6))
 LAST = ((), (4,), (), (1, 7, 0, 2, 6), (3, 5))
 
 MESH = pl.DeviceIdType.MESH
@@ -134,14 +134,15 @@
         )
         return first, second
 
-    leads = me == 0
-    follows = me != 0
+    lead = 0
+    leads = me == lead
+    follows = me != lead
     barrier = pltpu.get_barrier_semaphore()
 
     def greet(j):
         to = partner(j)
 
-        @pl.when(to != 0)
+        @pl.when(to != lead)
         def _():
             pl.semaphore_signal(
                 barrier, inc=1, device_id=(to, region), device_id_type=MESH
@@ -176,14 +177,14 @@
     def _():
         pl.semaphore_wait(barrier, others)
 
-    @pl.when(me == 1)
+    @pl.when(me == lead + 1)
     def _():
         pl.semaphore_signal(
-            group_in, inc=1, device_id=(0, region), device_id_type=MESH
+            group_in, inc=1, device_id=(lead, region), device_id_type=MESH
         )
         for side in (left, right):
             pl.semaphore_signal(
-                barrier, inc=1, device_id=(0, side), device_id_type=MESH
+                barrier, inc=1, device_id=(lead, side), device_id_type=MESH
             )
 
     @pl.when(leads)
@@ -406,7 +407,8 @@
 
     def iterate(step, carry):
         middle = split(middle_of(product()))
-        store(pl.ds(0, 2 * members), dot3((hi_ref[...], lo_ref[...]), middle))
+        for half_of in (top, bottom):
+            store(half_of, dot3((hi_ref[half_of], lo_ref[half_of]), middle))
         return carry
 
     lax.fori_loop(1, ITERS - 1, iterate, 0)
@@ -422,11 +424,23 @@
     take(xin.at[all_but_one], recv_sem.at[3])
     values = split(xin[...].reshape(members, xin.shape[2]))
     mean = mean_ref[...]
-    og[...] = (dot3(combined, values) + mean).reshape(og.shape)
     result_copy = exchange(
         4, lambda to: og.at[to], lambda slot: out_ref.at[:, slot, :]
     )
-    each(lambda j: result_copy(j).start())
+    for low in (0, n // 2):
+        rows = slice(low * group, low * group + half)
+        og[low : low + n // 2] = (
+            dot3([part[rows] for part in combined], values) + mean
+        ).reshape(n // 2, group, og.shape[2])
+
+        def send(j):
+            to = partner(j)
+
+            @pl.when((to >= low) & (to < low + n // 2))
+            def _():
+                result_copy(j).start()
+
+        each(send)
     own_result = pltpu.make_async_copy(
         og.at[me], out_ref.at[:, me, :], local_sem.at[2]
     )

time: 72 us -> 70.2 us (0.975)
  Pallas kernels: 70.8 us -> 69.1 us
    pallas_call x1, Pallas kernels: 70.8 us -> 69.1 us  [on_device(): pl.pallas_call(functools.partial(kernel, n, regions), out_shape=jax.Shape...]
where the time goes in v3:
time: 70.2 us; the launch traced here: 70.1 us
  Pallas kernels  69.1 us (98%)
  local copies, waits for them, and re-layouts  0.97 us (1%)
    pallas_call x1, Pallas kernels, on_device(): pl.pallas_call(functools.partial(kernel, n, regions), out_shape=jax.Shape...  69.1 us

profile of v3, /device:TPU:1, one launch (start us, length us, event | category | flops | bytes accessed | tf_op | source)
XLA Modules:
  0.0 70.1 jit_solution(3544663289454604669)
XLA Ops:
  0.0 69.1 %analysis.1 = f32[16,16,1024]{2,1,0:T(8,128)S(1)} custom-call(s32[16]{0:T(128)} %counts_in.1, s32[16,12]{1,0:T(8,128)} %lists_in.1, f32[16,8,256]{2,1,0:T(8,128)} %obs_in.1, f32[8,256]{1,0:T(8,128)} %depart_in.1, f32[8,256]{1,0:T(8,128)} %inv_in.1, f32[16,1024]{1,0:T(8,128)} %mean_in.1, f32[16,16,1024]{2,1,0:T(8,128)} %perturb_ref.1), custom_call_target="tpu_custom_call" | custom-call | tf_op jit(solution)/shard_map/analysis/pallas_call | solution.py:469
  69.1 1.0 %copy.9 = f32[16,16,1024]{2,1,0:T(8,128)} copy(f32[16,16,1024]{2,1,0:T(8,128)S(1)} %analysis.1) | data formatting | bytes 2097152

commit v4 on v3

--- a/solution.py
+++ b/solution.py
@@ -313,7 +313,7 @@
     for copy in extra_near:
         copy.start()
 
-    for ahead in chip_order:
+    for ahead in reversed(chip_order):
         take(cs.at[1, 0] if ahead else cs.at[1, 0, 0], chip_sem.at[ahead])
         b = lax.rem(chip - ahead + chips, chips)
         for copy in near(2, cs.at[1, b], cs.at[0, b], cs.at[2, b]):

time: 70.2 us -> 70.9 us (level)
  no operation moved by 1% of the time
where the time goes in v4:
time: 70.9 us; the launch traced here: 70.8 us
  Pallas kernels  69.8 us (98%)
  local copies, waits for them, and re-layouts  0.97 us (1%)
    pallas_call x1, Pallas kernels, on_device(): pl.pallas_call(functools.partial(kernel, n, regions), out_shape=jax.Shape...  69.8 us

profile of v4, /device:TPU:1, one launch (start us, length us, event | category | flops | bytes accessed | tf_op | source)
XLA Modules:
  0.0 70.8 jit_solution(11917570091956215947)
XLA Ops:
  0.0 69.8 %analysis.1 = f32[16,16,1024]{2,1,0:T(8,128)S(1)} custom-call(s32[16]{0:T(128)} %counts_in.1, s32[16,12]{1,0:T(8,128)} %lists_in.1, f32[16,8,256]{2,1,0:T(8,128)} %obs_in.1, f32[8,256]{1,0:T(8,128)} %depart_in.1, f32[8,256]{1,0:T(8,128)} %inv_in.1, f32[16,1024]{1,0:T(8,128)} %mean_in.1, f32[16,16,1024]{2,1,0:T(8,128)} %perturb_ref.1), custom_call_target="tpu_custom_call" | custom-call | tf_op jit(solution)/shard_map/analysis/pallas_call | solution.py:469
  69.8 1.0 %copy.9 = f32[16,16,1024]{2,1,0:T(8,128)} copy(f32[16,16,1024]{2,1,0:T(8,128)S(1)} %analysis.1) | data formatting | bytes 2097152

commit v5 on v3

--- a/solution.py
+++ b/solution.py
@@ -9,7 +9,7 @@
 
 ITERS = 6
 PLAN = ((), (4,), (2, 6), (1, 7, 0), (3, 5))
-FIRST = ((), (3, 5), (4, 1, 7, 0), (), (2, 6))
+FIRST = ((), (3, 5), (4, 2, 6), (), (1, 7, 0))
 LAST = ((), (4,), (), (1, 7, 0, 2, 6), (3, 5))
 
 MESH = pl.DeviceIdType.MESH
@@ -248,13 +248,15 @@
         extras = jnp.where(extra_lane == group + i, diagonal, extras)
     ex[1] = extras
 
-    def combine(values):
+    def combine(values, columns):
         top = values.astype(jnp.bfloat16)
         rest = values - top.astype(jnp.float32)
         middle = rest.astype(jnp.bfloat16)
         last = (rest - middle.astype(jnp.float32)).astype(jnp.bfloat16)
         parts = [
-            jnp.dot(chosen, part, preferred_element_type=jnp.float32)
+            jnp.dot(
+                chosen[:, columns], part, preferred_element_type=jnp.float32
+            )
             for part in (top, middle, last)
         ]
         return parts[0] + (parts[1] + parts[2])
@@ -320,19 +322,22 @@
             copy.start()
     send_background(3)
 
-    take(cs.at[0], near_recv.at[2])
-    take(cs.at[2], near_recv.at[3])
+    def slices(low, high):
+        return jnp.concatenate(
+            [
+                cs[low:high, :, i // 8, i % 8, :].reshape((high - low) * blocks, 128)
+                for i in range(group)
+            ],
+            axis=1,
+        )
+
     for copy in extra_near:
         copy.wait_recv()
-    sp[:, group, :] = combine(ex[...].reshape(3 * blocks, 128))
-    near_squares = jnp.concatenate(
-        [
-            cs[:, :, i // 8, i % 8, :].reshape(3 * blocks, 128)
-            for i in range(group)
-        ],
-        axis=1,
-    )
-    tile_squares = combine(near_squares)
+    sp[:, group, :] = combine(ex[...].reshape(3 * blocks, 128), slice(0, 3 * blocks))
+    take(cs.at[2], near_recv.at[3])
+    tile_squares = combine(slices(1, 3), slice(blocks, 3 * blocks))
+    take(cs.at[0], near_recv.at[2])
+    tile_squares = tile_squares + combine(slices(0, 1), slice(0, blocks))
     for i in range(group):
         sp[:, i, :] = tile_squares[:, i * 128 : (i + 1) * 128]
     used = pl.ds(0, group + 1)
@@ -412,11 +417,12 @@
         return carry
 
     lax.fori_loop(1, ITERS - 1, iterate, 0)
+    roots = (hi_ref[bottom], lo_ref[bottom])
+    carried = dot3(split(jnp.broadcast_to(vector, (8, members))), roots)
     middle = split(middle_of(product()))
-    inverse_root = dot3((hi_ref[bottom], lo_ref[bottom]), middle)
-    root_parts = split(inverse_root)
-    inner = dot3(split(jnp.broadcast_to(vector, (8, members))), root_parts)
-    shift = dot3(split(inner), root_parts)[0:1] * inverse_scale
+    inverse_root = dot3(roots, middle)
+    inner = dot3(split(carried), middle)
+    shift = dot3(split(inner), split(inverse_root))[0:1] * inverse_scale
     spread = jnp.sqrt((members - 1.0) * inverse_scale)
     combined = split(inverse_root * spread + shift)
 

time: 70.2 us -> 70 us (level)
  no operation moved by 1% of the time
where the time goes in v5:
time: 70 us; the launch traced here: 69.8 us
  Pallas kernels  68.8 us (98%)
  local copies, waits for them, and re-layouts  0.97 us (1%)
    pallas_call x1, Pallas kernels, on_device(): pl.pallas_call(functools.partial(kernel, n, regions), out_shape=jax.Shape...  68.8 us

profile of v5, /device:TPU:1, one launch (start us, length us, event | category | flops | bytes accessed | tf_op | source)
XLA Modules:
  0.0 69.8 jit_solution(9684052293989490959)
XLA Ops:
  0.0 68.8 %analysis.1 = f32[16,16,1024]{2,1,0:T(8,128)S(1)} custom-call(s32[16]{0:T(128)} %counts_in.1, s32[16,12]{1,0:T(8,128)} %lists_in.1, f32[16,8,256]{2,1,0:T(8,128)} %obs_in.1, f32[8,256]{1,0:T(8,128)} %depart_in.1, f32[8,256]{1,0:T(8,128)} %inv_in.1, f32[16,1024]{1,0:T(8,128)} %mean_in.1, f32[16,16,1024]{2,1,0:T(8,128)} %perturb_ref.1), custom_call_target="tpu_custom_call" | custom-call | tf_op jit(solution)/shard_map/analysis/pallas_call | solution.py:475
  68.8 1.0 %copy.9 = f32[16,16,1024]{2,1,0:T(8,128)} copy(f32[16,16,1024]{2,1,0:T(8,128)S(1)} %analysis.1) | data formatting | bytes 2097152
